TPU v7x, 512 devices: a whole 4x4x16 slice. The times are simulated.
512 devices in a mesh: group: 32 (over x, y, core), tile: 16 (over z).
Axes of the slice: x: 4, y: 4, z: 16, core: 2. Of those that a mesh axis runs over, the one named last changes fastest.
Arguments:
- block_input_frames: bfloat16 [32, 4, 16, 4, 8, 512], P('group', None, 'tile'), may hold values from -6 to 6
- norm_gain: float32 [512], replicated, may hold values from 0.25 to 1.75
- kernel: bfloat16 [3, 3, 3, 512, 512], P(None, None, None, 'group', 'tile'), may hold values from -0.0546875 to 0.0546875
- output_gradient: bfloat16 [32, 4, 16, 4, 8, 512], P('group', None, 'tile'), may hold values from -6 to 6
- group_count: int32 [32], P('group'), may hold values from 1 to 1, as said below
- clip_starts: int32 [32], P('group'), may hold values 0 or 1
Outputs:
- block_out: bfloat16 [32, 4, 16, 4, 8, 512], P('group', None, 'tile')
- input_grad: bfloat16 [32, 4, 16, 4, 8, 512], P('group', None, 'tile')
Inputs may be any that keep to these rules, and one draw needn't show every extreme that they name: `group_count`: each entry lies in 1 to 1, and some index of group holds 1 group.
All inputs are finite; a program needn't handle non-finite values. No bound on the sum of `clip_starts` on one device may be relied on, other than what follows from the above.
Results may differ from a plain program's by a relative error of at most 0.0045.
Values may be sent and summed in bfloat16 or wider, within the bound.
A program may use at most 64 MiB of HBM per device.

v0:
```python
import jax
import jax.numpy as jnp
from jax import lax
from jax.sharding import PartitionSpec as P

epsilon = 1e-06


def passed_along(value, axis, steps):
    count = lax.axis_size(axis)
    leading, last = (max(0, -steps), min(count, count - steps))
    return lax.ppermute(value, axis, [(source, source + steps) for source in range(leading, last)])


def normalize(field, gain):
    values = field.astype(jnp.float32)
    scale = lax.rsqrt(jnp.mean(values * values, axis=-1, keepdims=True) + epsilon)
    normed = values * scale * gain
    return (values, scale, normed)


def norm_grad(values, scale, normed, gain, upstream):
    sigma = jax.nn.sigmoid(normed)
    through = upstream * sigma * (1.0 + normed * (1.0 - sigma)) * gain
    cubed = scale * scale * scale
    return scale * through - values * cubed * jnp.mean(values * through, axis=-1, keepdims=True)


def conv_taps(padded, kernel, frame_count, height, width, backward):
    channels = padded.shape[4]
    accumulated = jnp.zeros((padded.shape[0] * frame_count * height * width, channels), jnp.float32)
    for step_t in range(3):
        for step_i in range(3):
            for step_j in range(3):
                window_view = padded[
                    :,
                    step_t : step_t + frame_count,
                    step_i : step_i + height,
                    step_j : step_j + width,
                    :,
                ]
                window_view = window_view.reshape(-1, channels)
                if backward:
                    kernel_tap = kernel[2 - step_t, 2 - step_i, 2 - step_j].T
                else:
                    kernel_tap = kernel[step_t, step_i, step_j]
                accumulated = accumulated + jnp.dot(
                    window_view, kernel_tap, preferred_element_type=jnp.float32
                )
    return accumulated.reshape(padded.shape[0], frame_count, height, width, channels)


def spatial_halo(field):
    tile_columns = min(lax.axis_size("tile"), 4)
    place = lax.axis_index("tile") % tile_columns
    left_keep = (place != 0).astype(field.dtype)
    right_keep = (place != tile_columns - 1).astype(field.dtype)
    vertical = []
    for shift_by, edge_part in ((tile_columns, field[:, :, -1:]), (-tile_columns, field[:, :, :1])):
        vertical.append(passed_along(edge_part, "tile", shift_by))
    stacked = jnp.concatenate([vertical[0], field, vertical[1]], axis=2)
    sideways = []
    for shift_by, edge_part in ((1, stacked[:, :, :, -1:]), (-1, stacked[:, :, :, :1])):
        sideways.append(passed_along(edge_part, "tile", shift_by))
    left_side = sideways[0] * left_keep
    right_side = sideways[1] * right_keep
    return jnp.concatenate([left_side, stacked, right_side], axis=3)


def per_device(block_input_frames, norm_gain, kernel, output_gradient, group_count, clip_starts):
    frames_here = block_input_frames[:, :, 0]
    slot_count, frame_count, height, width, channels = frames_here.shape
    partial_kernel = lax.all_gather(kernel, "group", axis=3, tiled=True)
    full_kernel = lax.all_gather(partial_kernel, "tile", axis=4, tiled=True)
    slot_indices = jnp.arange(slot_count, dtype=jnp.int32)
    count_here = group_count[0]
    position = lax.axis_index("group")
    live_mask = slot_indices < count_here
    has_source = live_mask & (clip_starts == 0) & ((slot_indices > 0) | (position > 0))
    live_wide = live_mask[:, None, None, None, None]
    source_wide = has_source[:, None, None, None, None]
    values, scale, normed = normalize(frames_here, norm_gain)
    activated = (normed * jax.nn.sigmoid(normed)).astype(jnp.bfloat16)
    tails = activated[:, frame_count - 2 :]
    last_tail = lax.dynamic_index_in_dim(tails, count_here - 1, 0, keepdims=False)
    arrived = passed_along(last_tail, "group", 1)
    earlier = jnp.concatenate([arrived[None], tails[:-1]], axis=0)
    cache = jnp.where(source_wide, earlier, jnp.zeros_like(earlier))
    extended = jnp.concatenate([cache, activated], axis=1)
    padded = spatial_halo(extended)
    mixed = conv_taps(padded, full_kernel, frame_count, height, width, False)
    block_out = jnp.where(live_wide, values + mixed, jnp.float32(0.0)).astype(jnp.bfloat16)
    masked_grad = jnp.where(live_wide, output_gradient[:, :, 0], jnp.zeros_like(frames_here))
    grad_halo = spatial_halo(masked_grad)
    grad_padded = jnp.pad(grad_halo, ((0, 0), (2, 2), (0, 0), (0, 0), (0, 0)))
    spread = conv_taps(grad_padded, full_kernel, frame_count + 2, height, width, True)
    heads = jnp.where(source_wide, spread[:, :2], jnp.float32(0.0))
    returned = passed_along(heads[0].astype(jnp.bfloat16), "group", -1).astype(jnp.float32)
    from_next = jnp.concatenate([heads[1:], jnp.zeros_like(heads)], axis=0)
    last_wide = (slot_indices == count_here - 1)[:, None, None, None, None]
    tail_grad = from_next + jnp.where(last_wide, returned[None], jnp.float32(0.0))
    upstream = jnp.concatenate(
        [spread[:, 2:frame_count], spread[:, frame_count:] + tail_grad], axis=1
    )
    gradient = masked_grad.astype(jnp.float32) + norm_grad(
        values, scale, normed, norm_gain, upstream
    )
    input_grad = jnp.where(live_wide, gradient, jnp.float32(0.0)).astype(jnp.bfloat16)
    return (block_out[:, :, None], input_grad[:, :, None])


def solution(mesh):
    placed = (
        P("group", None, "tile", None, None, None),
        P(),
        P(None, None, None, "group", "tile"),
        P("group", None, "tile", None, None, None),
        P("group"),
        P("group"),
    )
    return jax.shard_map(
        per_device,
        mesh=mesh,
        in_specs=placed,
        out_specs=(
            P("group", None, "tile", None, None, None),
            P("group", None, "tile", None, None, None),
        ),
        check_vma=False,
    )
```

profile of v0, /device:TPU:68, one launch (start us, length us, event | category | flops | bytes accessed | tf_op | source)
XLA Modules:
  0.0 287.6 jit_solution(16782991085841116728)
XLA Ops:
  7.2 31.5 %all_gather.6 = bf16[3,3,3,512,32]{4,3,2,1,0:T(8,128)(2,1)S(1)} all-gather(bf16[3,3,3,16,32]{4,3,2,1,0:T(8,128)(2,1)} %param.8), channel_id=1, replica_groups=mesh['group'=32,'tile'=16] {'group'}, dimensions={3}, use_global_device_ids=true | all-gather | bytes 912384 | tf_op jit(solution)/shard_map/all_gather | solution.py:73
  38.8 2.3 copy.23
  41.8 0.9 fusion.46
  42.7 9.1 %collective-permute-start.5 = (bf16[1,4,1,8,512]{4,3,2,1,0:T(8,128)(2,1)S(1)}, bf16[1,4,1,8,512]{4,3,2,1,0:T(8,128)(2,1)S(1)}, u32[]{:S(2)}, u32[]{:S(2)}) collective-permute-start(bf16[1,4,1,8,512]{4,3,2,1,0:T(8,128)(2,1)S(1)} %get-tuple-element.72), channel_id=1, source_target_pairs={{0,4},{1,5},{2,6},{3,7},{4,8},{5,9},{6,10},{7,11},{8,12},{9,13},{1... | collective-permute-start | bytes 98312 | tf_op jit(solution)/shard_map/ppermute | solution.py:12
  51.8 1.3 collective-permute-start.6
  53.1 1.0 fusion.31
  54.1 7.4 %collective-permute-done.6 = bf16[1,4,1,8,512]{4,3,2,1,0:T(8,128)(2,1)S(1)} collective-permute-done((bf16[1,4,1,8,512]{4,3,2,1,0:T(8,128)(2,1)S(1)}, bf16[1,4,1,8,512]{4,3,2,1,0:T(8,128)(2,1)S(1)}, u32[]{:S(2)}, u32[]{:S(2)}) %collective-permute-start.6) | collective-permute-done | bytes 32800 | tf_op jit(solution)/shard_map/ppermute | solution.py:12
  61.6 3.8 %collective-permute-start.7 = (bf16[1,4,6,1,512]{4,3,2,1,0:T(2,128)(2,1)S(1)}, bf16[1,4,6,1,512]{4,3,2,1,0:T(2,128)(2,1)S(1)}, u32[]{:S(2)}, u32[]{:S(2)}) collective-permute-start(bf16[1,4,6,1,512]{4,3,2,1,0:T(2,128)(2,1)S(1)} %get-tuple-element.60), channel_id=1, source_target_pairs={{0,1},{1,2},{2,3},{3,4},{4,5},{5,6},{6,7},{7,8},{8,9},{9,10},{10,1... | collective-permute-start | bytes 73736 | tf_op jit(solution)/shard_map/ppermute | solution.py:12
  66.1 2.0 collective-permute-start.8
  68.2 0.4 collective-permute-done.7
  68.7 6.6 %collective-permute-done.8 = bf16[1,4,6,1,512]{4,3,2,1,0:T(2,128)(2,1)S(1)} collective-permute-done((bf16[1,4,6,1,512]{4,3,2,1,0:T(2,128)(2,1)S(1)}, bf16[1,4,6,1,512]{4,3,2,1,0:T(2,128)(2,1)S(1)}, u32[]{:S(2)}, u32[]{:S(2)}) %collective-permute-start.8) | collective-permute-done | bytes 24608 | tf_op jit(solution)/shard_map/ppermute | solution.py:12
  75.8 1.6 fusion.50
  77.5 128.6 %all-gather.2.cloned.1.call-done = bf16[3,3,3,512,512]{3,4,2,1,0:T(8,128)(2,1)} async-done(((bf16[3,3,3,512,32]{3,4,2,1,0:T(8,128)(2,1)}), bf16[3,3,3,512,512]{3,4,2,1,0:T(8,128)(2,1)}) %all-gather.2.cloned.1.call-update) | async-done | bytes 14155792 | tf_op jit(solution)/shard_map/all_gather | solution.py:74
  206.1 1.5 fusion.7
  207.5 1.9 convolution_add_fusion.25
  209.5 2.1 convolution_add_fusion.24
  211.6 1.3 convolution_add_fusion.23
  212.9 1.3 convolution_add_fusion.22
  214.2 1.3 convolution_add_fusion.21
  215.5 1.3 convolution_add_fusion.20
  216.8 1.3 convolution_add_fusion.19
  218.2 1.4 convolution_add_fusion.18
  219.6 1.4 convolution_add_fusion.17
  221.0 1.2 convolution_add_fusion.16
  226.7 4.1 %collective-permute-start.9 = (bf16[2,4,8,512]{3,2,1,0:T(8,128)(2,1)S(1)}, bf16[2,4,8,512]{3,2,1,0:T(8,128)(2,1)S(1)}, u32[]{:S(2)}, u32[]{:S(2)}) collective-permute-start(bf16[2,4,8,512]{3,2,1,0:T(8,128)(2,1)S(1)} %fusion.47), channel_id=1, source_target_pairs={{16,0},{32,16},{48,32},{64,48},{80,64},{96,80},{112,96},{128,112},... | collective-permute-start | bytes 196616 | tf_op jit(solution)/shard_map/ppermute | solution.py:12
  231.0 1.7 collective-permute-done.9
  232.7 0.3 fusion.43
  233.0 1.9 collective-permute-start
  235.0 5.8 %collective-permute-done = bf16[2,4,8,512]{3,2,1,0:T(8,128)(2,1)S(1)} collective-permute-done((bf16[2,4,8,512]{3,2,1,0:T(8,128)(2,1)S(1)}, bf16[2,4,8,512]{3,2,1,0:T(8,128)(2,1)S(1)}, u32[]{:S(2)}, u32[]{:S(2)}) %collective-permute-start) | collective-permute-done | bytes 65568 | tf_op jit(solution)/shard_map/ppermute | solution.py:12
  240.8 7.6 %collective-permute-start.1 = (bf16[1,6,1,8,512]{4,3,2,1,0:T(8,128)(2,1)S(1)}, bf16[1,6,1,8,512]{4,3,2,1,0:T(8,128)(2,1)S(1)}, u32[]{:S(2)}, u32[]{:S(2)}) collective-permute-start(bf16[1,6,1,8,512]{4,3,2,1,0:T(8,128)(2,1)S(1)} %get-tuple-element.66), channel_id=1, source_target_pairs={{0,4},{1,5},{2,6},{3,7},{4,8},{5,9},{6,10},{7,11},{8,12},{9,13},{1... | collective-permute-start | bytes 147464 | tf_op jit(solution)/shard_map/ppermute | solution.py:12
  248.5 1.3 collective-permute-start.2
  249.8 1.3 collective-permute-done.1
  251.2 7.2 %collective-permute-done.2 = bf16[1,6,1,8,512]{4,3,2,1,0:T(8,128)(2,1)S(1)} collective-permute-done((bf16[1,6,1,8,512]{4,3,2,1,0:T(8,128)(2,1)S(1)}, bf16[1,6,1,8,512]{4,3,2,1,0:T(8,128)(2,1)S(1)}, u32[]{:S(2)}, u32[]{:S(2)}) %collective-permute-start.2) | collective-permute-done | bytes 49184 | tf_op jit(solution)/shard_map/ppermute | solution.py:12
  258.5 5.9 %collective-permute-start.3 = (bf16[1,6,6,1,512]{4,3,2,1,0:T(2,128)(2,1)S(1)}, bf16[1,6,6,1,512]{4,3,2,1,0:T(2,128)(2,1)S(1)}, u32[]{:S(2)}, u32[]{:S(2)}) collective-permute-start(bf16[1,6,6,1,512]{4,3,2,1,0:T(2,128)(2,1)S(1)} %get-tuple-element.53), channel_id=1, source_target_pairs={{0,1},{1,2},{2,3},{3,4},{4,5},{5,6},{6,7},{7,8},{8,9},{9,10},{10,1... | collective-permute-start | bytes 110600 | tf_op jit(solution)/shard_map/ppermute | solution.py:12
  264.4 2.1 collective-permute-start.4
  266.7 3.9 %collective-permute-done.4 = bf16[1,6,6,1,512]{4,3,2,1,0:T(2,128)(2,1)S(1)} collective-permute-done((bf16[1,6,6,1,512]{4,3,2,1,0:T(2,128)(2,1)S(1)}, bf16[1,6,6,1,512]{4,3,2,1,0:T(2,128)(2,1)S(1)}, u32[]{:S(2)}, u32[]{:S(2)}) %collective-permute-start.4) | collective-permute-done | bytes 36896 | tf_op jit(solution)/shard_map/ppermute | solution.py:12
  270.7 0.3 pad_maximum_fusion
  271.6 0.3 convolution_add_fusion.51
  272.0 0.3 convolution_add_fusion.50
  272.3 0.3 convolution_add_fusion.49
  272.6 0.3 convolution_add_fusion.48
  272.9 0.3 convolution_add_fusion.47
  273.2 0.3 convolution_add_fusion.46
  273.5 0.3 convolution_add_fusion.45
  273.9 0.3 convolution_add_fusion.44
  274.2 0.3 convolution_add_fusion.43
  274.5 0.3 convolution_add_fusion.42
  274.8 0.3 convolution_add_fusion.41
  275.1 0.3 convolution_add_fusion.40
  275.4 0.3 convolution_add_fusion.39
  275.7 0.3 convolution_add_fusion.38
  276.0 0.3 convolution_add_fusion.37
  276.3 0.3 convolution_add_fusion.36
  276.7 0.3 convolution_add_fusion.35
  277.0 0.3 convolution_add_fusion.34
  277.3 0.3 convolution_add_fusion.33
  277.6 0.3 convolution_add_fusion.32
  277.9 0.3 convolution_add_fusion.31
  278.2 0.3 convolution_add_fusion.30
  278.5 0.3 convolution_add_fusion.29
  278.8 0.3 convolution_add_fusion.28
  279.1 0.3 convolution_add_fusion.27
  279.5 0.3 convolution_add_fusion.26
  279.8 0.9 fusion.30
  (62 shorter events, 6.2 us)
Async XLA Ops:
  7.2 198.9 %all-gather.2.cloned.1.call-start = ((), (), s32[]{:S(2)}) async-start(), calls=%async_computation | async-start | bytes 15040512 | tf_op jit(solution)/shard_map/all_gather | solution.py:74
  42.7 11.4 %collective-permute-start.5 = (bf16[1,4,1,8,512]{4,3,2,1,0:T(8,128)(2,1)S(1)}, bf16[1,4,1,8,512]{4,3,2,1,0:T(8,128)(2,1)S(1)}, u32[]{:S(2)}, u32[]{:S(2)}) collective-permute-start(bf16[1,4,1,8,512]{4,3,2,1,0:T(8,128)(2,1)S(1)} %get-tuple-element.72), channel_id=1, source_target_pairs={{0,4},{1,5},{2,6},{3,7},{4,8},{5,9},{6,10},{7,11},{8,12},{9,13},{1... | collective-permute-start | bytes 98312 | tf_op jit(solution)/shard_map/ppermute | solution.py:12
  51.8 9.7 %collective-permute-start.6 = (bf16[1,4,1,8,512]{4,3,2,1,0:T(8,128)(2,1)S(1)}, bf16[1,4,1,8,512]{4,3,2,1,0:T(8,128)(2,1)S(1)}, u32[]{:S(2)}, u32[]{:S(2)}) collective-permute-start(bf16[1,4,1,8,512]{4,3,2,1,0:T(8,128)(2,1)S(1)} %get-tuple-element.73), channel_id=1, source_target_pairs={{4,0},{5,1},{6,2},{7,3},{8,4},{9,5},{10,6},{11,7},{12,8},{13,9},{1... | collective-permute-start | bytes 98312 | tf_op jit(solution)/shard_map/ppermute | solution.py:12
  61.6 7.0 %collective-permute-start.7 = (bf16[1,4,6,1,512]{4,3,2,1,0:T(2,128)(2,1)S(1)}, bf16[1,4,6,1,512]{4,3,2,1,0:T(2,128)(2,1)S(1)}, u32[]{:S(2)}, u32[]{:S(2)}) collective-permute-start(bf16[1,4,6,1,512]{4,3,2,1,0:T(2,128)(2,1)S(1)} %get-tuple-element.60), channel_id=1, source_target_pairs={{0,1},{1,2},{2,3},{3,4},{4,5},{5,6},{6,7},{7,8},{8,9},{9,10},{10,1... | collective-permute-start | bytes 73736 | tf_op jit(solution)/shard_map/ppermute | solution.py:12
  66.1 9.2 %collective-permute-start.8 = (bf16[1,4,6,1,512]{4,3,2,1,0:T(2,128)(2,1)S(1)}, bf16[1,4,6,1,512]{4,3,2,1,0:T(2,128)(2,1)S(1)}, u32[]{:S(2)}, u32[]{:S(2)}) collective-permute-start(bf16[1,4,6,1,512]{4,3,2,1,0:T(2,128)(2,1)S(1)} %get-tuple-element.61), channel_id=1, source_target_pairs={{1,0},{2,1},{3,2},{4,3},{5,4},{6,5},{7,6},{8,7},{9,8},{10,9},{11,1... | collective-permute-start | bytes 73736 | tf_op jit(solution)/shard_map/ppermute | solution.py:12
  206.1 15.0 %copy-start = (bf16[3,3,3,512,512]{3,4,2,1,0:T(8,128)(2,1)S(1)}, bf16[3,3,3,512,512]{3,4,2,1,0:T(8,128)(2,1)}, u32[]{:S(2)}) copy-start(bf16[3,3,3,512,512]{3,4,2,1,0:T(8,128)(2,1)} %all-gather.2.cloned.1.call-done) | copy-start | bytes 42467332
  206.1 16.2 %copy-start.7 = (bf16[1,6,4,8,512]{4,3,2,1,0:T(8,128)(2,1)S(1)}, bf16[1,6,4,8,512]{4,3,2,1,0:T(8,128)(2,1)}, u32[]{:S(2)}) copy-start(bf16[1,6,4,8,512]{4,3,2,1,0:T(8,128)(2,1)} %get-tuple-element.17) | copy-start | bytes 589828
  206.1 16.5 %copy-start.6 = (bf16[1,6,4,8,512]{4,3,2,1,0:T(8,128)(2,1)S(1)}, bf16[1,6,4,8,512]{4,3,2,1,0:T(8,128)(2,1)}, u32[]{:S(2)}) copy-start(bf16[1,6,4,8,512]{4,3,2,1,0:T(8,128)(2,1)} %get-tuple-element.16) | copy-start | bytes 589828
  206.1 16.8 %copy-start.5 = (bf16[1,6,4,8,512]{4,3,2,1,0:T(8,128)(2,1)S(1)}, bf16[1,6,4,8,512]{4,3,2,1,0:T(8,128)(2,1)}, u32[]{:S(2)}) copy-start(bf16[1,6,4,8,512]{4,3,2,1,0:T(8,128)(2,1)} %get-tuple-element.15) | copy-start | bytes 589828
  206.1 17.0 %copy-start.4 = (bf16[1,6,4,8,512]{4,3,2,1,0:T(8,128)(2,1)S(1)}, bf16[1,6,4,8,512]{4,3,2,1,0:T(8,128)(2,1)}, u32[]{:S(2)}) copy-start(bf16[1,6,4,8,512]{4,3,2,1,0:T(8,128)(2,1)} %get-tuple-element.14) | copy-start | bytes 589828
  206.1 17.3 %copy-start.3 = (bf16[1,6,4,8,512]{4,3,2,1,0:T(8,128)(2,1)S(1)}, bf16[1,6,4,8,512]{4,3,2,1,0:T(8,128)(2,1)}, u32[]{:S(2)}) copy-start(bf16[1,6,4,8,512]{4,3,2,1,0:T(8,128)(2,1)} %get-tuple-element.13) | copy-start | bytes 589828
  206.1 17.6 %copy-start.2 = (bf16[1,6,4,8,512]{4,3,2,1,0:T(8,128)(2,1)S(1)}, bf16[1,6,4,8,512]{4,3,2,1,0:T(8,128)(2,1)}, u32[]{:S(2)}) copy-start(bf16[1,6,4,8,512]{4,3,2,1,0:T(8,128)(2,1)} %get-tuple-element.12) | copy-start | bytes 589828
  218.1 12.6 %copy-start.1 = (bf16[1,4,1,4,8,512]{5,4,3,2,1,0:T(8,128)(2,1)S(1)}, bf16[1,4,1,4,8,512]{5,4,3,2,1,0:T(8,128)(2,1)}, u32[]{:S(2)}) copy-start(bf16[1,4,1,4,8,512]{5,4,3,2,1,0:T(8,128)(2,1)} %param.6) | copy-start | bytes 393220
  218.2 12.6 %copy-start.9 = (f32[512]{0:T(512)S(1)}, f32[512]{0:T(512)}, u32[]{:S(2)}) copy-start(f32[512]{0:T(512)} %param.7) | copy-start | bytes 6148
  226.7 6.0 %collective-permute-start.9 = (bf16[2,4,8,512]{3,2,1,0:T(8,128)(2,1)S(1)}, bf16[2,4,8,512]{3,2,1,0:T(8,128)(2,1)S(1)}, u32[]{:S(2)}, u32[]{:S(2)}) collective-permute-start(bf16[2,4,8,512]{3,2,1,0:T(8,128)(2,1)S(1)} %fusion.47), channel_id=1, source_target_pairs={{16,0},{32,16},{48,32},{64,48},{80,64},{96,80},{112,96},{128,112},... | collective-permute-start | bytes 196616 | tf_op jit(solution)/shard_map/ppermute | solution.py:12
  233.0 7.7 %collective-permute-start = (bf16[2,4,8,512]{3,2,1,0:T(8,128)(2,1)S(1)}, bf16[2,4,8,512]{3,2,1,0:T(8,128)(2,1)S(1)}, u32[]{:S(2)}, u32[]{:S(2)}) collective-permute-start(bf16[2,4,8,512]{3,2,1,0:T(8,128)(2,1)S(1)} %slice_bitcast_fusion.81), channel_id=1, source_target_pairs={{0,16},{16,32},{32,48},{48,64},{64,80},{80,96},{96,112},{112,128},... | collective-permute-start | bytes 196616 | tf_op jit(solution)/shard_map/ppermute | solution.py:12
  240.8 10.3 %collective-permute-start.1 = (bf16[1,6,1,8,512]{4,3,2,1,0:T(8,128)(2,1)S(1)}, bf16[1,6,1,8,512]{4,3,2,1,0:T(8,128)(2,1)S(1)}, u32[]{:S(2)}, u32[]{:S(2)}) collective-permute-start(bf16[1,6,1,8,512]{4,3,2,1,0:T(8,128)(2,1)S(1)} %get-tuple-element.66), channel_id=1, source_target_pairs={{0,4},{1,5},{2,6},{3,7},{4,8},{5,9},{6,10},{7,11},{8,12},{9,13},{1... | collective-permute-start | bytes 147464 | tf_op jit(solution)/shard_map/ppermute | solution.py:12
  248.5 9.9 %collective-permute-start.2 = (bf16[1,6,1,8,512]{4,3,2,1,0:T(8,128)(2,1)S(1)}, bf16[1,6,1,8,512]{4,3,2,1,0:T(8,128)(2,1)S(1)}, u32[]{:S(2)}, u32[]{:S(2)}) collective-permute-start(bf16[1,6,1,8,512]{4,3,2,1,0:T(8,128)(2,1)S(1)} %get-tuple-element.67), channel_id=1, source_target_pairs={{4,0},{5,1},{6,2},{7,3},{8,4},{9,5},{10,6},{11,7},{12,8},{13,9},{1... | collective-permute-start | bytes 147464 | tf_op jit(solution)/shard_map/ppermute | solution.py:12
  258.5 8.2 %collective-permute-start.3 = (bf16[1,6,6,1,512]{4,3,2,1,0:T(2,128)(2,1)S(1)}, bf16[1,6,6,1,512]{4,3,2,1,0:T(2,128)(2,1)S(1)}, u32[]{:S(2)}, u32[]{:S(2)}) collective-permute-start(bf16[1,6,6,1,512]{4,3,2,1,0:T(2,128)(2,1)S(1)} %get-tuple-element.53), channel_id=1, source_target_pairs={{0,1},{1,2},{2,3},{3,4},{4,5},{5,6},{6,7},{7,8},{8,9},{9,10},{10,1... | collective-permute-start | bytes 110600 | tf_op jit(solution)/shard_map/ppermute | solution.py:12
  264.4 6.2 %collective-permute-start.4 = (bf16[1,6,6,1,512]{4,3,2,1,0:T(2,128)(2,1)S(1)}, bf16[1,6,6,1,512]{4,3,2,1,0:T(2,128)(2,1)S(1)}, u32[]{:S(2)}, u32[]{:S(2)}) collective-permute-start(bf16[1,6,6,1,512]{4,3,2,1,0:T(2,128)(2,1)S(1)} %get-tuple-element.52), channel_id=1, source_target_pairs={{1,0},{2,1},{3,2},{4,3},{5,4},{6,5},{7,6},{8,7},{9,8},{10,9},{11,1... | collective-permute-start | bytes 110600 | tf_op jit(solution)/shard_map/ppermute | solution.py:12
  272.3 7.5 %copy-start.8 = (bf16[1,4,1,4,8,512]{5,4,3,2,1,0:T(8,128)(2,1)S(1)}, bf16[1,4,1,4,8,512]{5,4,3,2,1,0:T(8,128)(2,1)}, u32[]{:S(2)}) copy-start(bf16[1,4,1,4,8,512]{5,4,3,2,1,0:T(8,128)(2,1)} %param.9) | copy-start | bytes 393220
Sparse Core Ops, SparseCore 0:
  41.2 164.7 all-gather.1
where the time goes:
time: 289 us; the launch traced here: 288 us
  waiting for transfers between devices  163 us (56%)
  starting transfers between devices  39.2 us (14%)
  blocking collectives  31.5 us (11%)
  matrix products  28.5 us (10%)
  between operations  16.1 us (6%)
  local copies, waits for them, and re-layouts  4.57 us (2%)
  other arithmetic  4.5 us (2%)
    all_gather x1, waiting for transfers between devices, per_device(): full_kernel = lax.all_gather(partial_kernel, 'tile', axis=4, tiled=True)  129 us
    ppermute x10, starting transfers between devices, passed_along(): lax.ppermute(value, axis, [(source, source + steps) for source in range(l...  39.2 us
    ppermute x10, waiting for transfers between devices, passed_along(): lax.ppermute(value, axis, [(source, source + steps) for source in range(l...  34.5 us
    all_gather x1, blocking collectives, per_device(): partial_kernel = lax.all_gather(kernel, 'group', axis=3, tiled=True)  31.5 us
    dot_general x54, matrix products, conv_taps(): jnp.dot(window_view, kernel_tap, preferred_element_type=jnp.float32)  28.5 us
  transfers between devices with their start and end apart: 11, of which 9 were waited for; matrix products, arithmetic and copies ran while one was open for 2% of the time, Pallas kernels for 0%

commit v1 on v0

v1 whole, which is shorter than its diff:
```python
import numpy as np
import jax
import jax.numpy as jnp
from jax import lax
from jax.experimental import pallas as pl
from jax.experimental.pallas import tpu as pltpu
from jax.sharding import PartitionSpec as P

MESH = pl.DeviceIdType.MESH
EPSILON = 1e-06
F32, BF16 = jnp.float32, jnp.bfloat16


def swap_table():
    table = np.zeros((512, 512), np.float32)
    for a in range(4):
        for b in range(4):
            for o in range(32):
                table[a * 128 + b * 32 + o, b * 128 + a * 32 + o] = 1
    return table.reshape(512, 4, 128).transpose(1, 0, 2)


def column_table():
    table = np.zeros((32, 128), np.float32)
    for it in range(16):
        table[it, it * 8 + 7] = 1
        table[16 + it, it * 8] = 1
    return table


def corner_table():
    table = np.zeros((4, 64, 128), np.float32)
    for k in range(4):
        for corner, (i, j) in enumerate(((3, 7), (3, 0), (0, 7), (0, 0))):
            for t in range(4):
                table[k, 16 * corner + 4 * k + t, (i * 4 + t) * 8 + j] = 1
    return table


def edge_table():
    table = np.zeros((4, 64, 128), np.float32)
    for k in range(4):
        for side in range(2):
            for t in range(4):
                first = 16 * t + 8 * side
                table[k, first, 32 + 16 * side + 4 * k + t] = 1
                table[k, first + 5, 64 + 16 * side + 4 * k + t] = 1
                for i in range(4):
                    table[k, first + 1 + i, 16 * side + i * 4 + t] = 1
    return table


SHARDS = (0, -1, 7, -4, -7, 4, 1, -2, 6, -5, -8, 3, -3, -6, 5, 2)
CHUNKS = ((0, 1, 0), (1, 3, 0), (4, 3, 1), (7, 5, 0), (12, 4, 1))
STRIP_STEPS, COLUMN_STEPS, CORNER_STEPS = (4, -4), (1, -1), (5, 3, -3, -5)


def dot(left, right):
    return jnp.dot(left, right, preferred_element_type=F32)


def swap_lanes(value, swap_ref):
    return dot(value, jnp.concatenate([swap_ref[k] for k in range(4)], axis=1))


def body(
    x_hbm, gain_hbm, w_hbm, g_hbm, count_ref, starts_ref, swap_hbm, column_hbm, corner_hbm, edge_hbm,
    out_ref, grad_ref,
    xv, gainv, wv, gv, swap_ref, column_pick, corner_pick, edge_pick,
    wz, wbuf, tsend, trecv, rows_s, rows_r, corners_s, corners_r, amsg, abuf, gb, fbuf, bbuf,
    acc_f, acc_b, psend, precv, bsend, brecv, dsend, drecv, mix,
    in_s, z_s, z_r, t_s, t_r, h_s, h_r, a_s, a_r, gy_s, gy_r,
    wx_s, wx_r, wf_s, wf_r, wc_s, wc_r, p_s, p_r, b_s, b_r, d_s, d_r,
):
    loads = [
        pltpu.make_async_copy(src, dst, in_s.at[k])
        for k, (src, dst) in enumerate(
            (
                (w_hbm, wv), (g_hbm, gv), (x_hbm, xv), (gain_hbm, gainv), (swap_hbm, swap_ref),
                (column_hbm, column_pick), (corner_hbm, corner_pick), (edge_hbm, edge_pick),
            )
        )
    ]
    for load in loads:
        load.start()

    group = lax.axis_index("group")
    z = lax.axis_index("tile")
    x, y, c = lax.div(group, 8), lax.rem(lax.div(group, 2), 4), lax.rem(group, 2)

    def device(x_at, y_at, c_at, z_at):
        return (x_at * 8 + y_at * 2 + c_at, z_at)

    def mod4(value):
        return lax.rem(value + 4, 4)

    def zmove(step):
        return (group, lax.rem(z + step + 16, 16))

    core = device(x, y, 1 - c, z)
    x_right, x_left = device(mod4(x + 1), y, c, z), device(mod4(x - 1), y, c, z)
    y_peers = [device(x, mod4(y + d), c, z) for d in (1, 2, 3)]
    y_right, y_left = y_peers[0], y_peers[2]
    following, previous = lax.rem(group + 1, 32), lax.rem(group + 31, 32)
    after, before = (following, z), (previous, z)
    head_targets = [(lax.rem(x * 8 + 2 * k + c + 31, 32), z) for k in range(4)]
    head_sources = [device(lax.div(following, 8), k, lax.rem(following, 2), z) for k in range(4)]

    barrier = pltpu.get_barrier_semaphore()
    partners = [core, x_right, x_left, *y_peers, after, before, *head_sources]
    partners += [zmove(step) for step in STRIP_STEPS + COLUMN_STEPS + CORNER_STEPS + (7, -7)]
    for partner in partners:
        pl.semaphore_signal(barrier, inc=1, device_id=partner, device_id_type=MESH)

    started = []

    def remote(src, dst, send_sem, recv_sem, target):
        return pltpu.make_async_remote_copy(
            src_ref=src, dst_ref=dst, send_sem=send_sem, recv_sem=recv_sem, device_id=target, device_id_type=MESH
        )

    def send(src, dst, send_sem, recv_sem, target):
        copy = remote(src, dst, send_sem, recv_sem, target)
        copy.start()
        started.append(copy)

    def arrived(dst, sem):
        remote(dst, dst, sem, sem, core).wait_recv()

    def z_first():
        for k, step in enumerate(SHARDS[1:7]):
            send(wz.at[x, 0], wz.at[x, 1 + k], z_s.at[k], z_r.at[k], zmove(-step))

    def z_first_wait():
        for k in range(6):
            arrived(wz.at[x, 1 + k], z_r.at[k])

    def z_second():
        send(wz.at[x, pl.ds(1, 5)], wz.at[x, pl.ds(7, 5)], z_s.at[6], z_r.at[6], zmove(1))
        send(wz.at[x, pl.ds(3, 4)], wz.at[x, pl.ds(12, 4)], z_s.at[7], z_r.at[7], zmove(-1))

    def z_second_wait():
        arrived(wz.at[x, pl.ds(7, 5)], z_r.at[6])
        arrived(wz.at[x, pl.ds(12, 4)], z_r.at[7])

    def x_block(step, k):
        return wz.at[mod4(x + step), pl.ds(CHUNKS[k][0], CHUNKS[k][1])]

    def x_send(k, side):
        block = x_block(0, k)
        send(block, block, wx_s.at[side, k], wx_r.at[side, k], x_left if side else x_right)

    def x_arrived(k, side):
        arrived(x_block(1 if side else -1, k), wx_r.at[side, k])

    def x_pass(k):
        side = CHUNKS[k][2]
        x_arrived(k, side)
        block = x_block(1 if side else -1, k)
        send(block, block, wf_s.at[k], wf_r.at[k], x_left if side else x_right)

    def x_far(k):
        arrived(x_block(2, k), wf_r.at[k])

    places = []
    for shard in range(16):
        away = lax.rem(shard - z + 24, 16) - 8
        place = jnp.int32(0)
        for slot in range(1, 16):
            place = jnp.where(away == SHARDS[slot], slot, place)
        places.append(place)

    def w_layout(step):
        at = mod4(x + step)
        rows = []
        for quad in range(4):
            rows.append(jnp.concatenate([wz[at, places[quad * 4 + j]] for j in range(4)], axis=1))
        full = swap_lanes(jnp.concatenate(rows, axis=0), swap_ref).astype(BF16)
        for quad in range(4):
            for tap in range(27):
                row, lanes = quad * 112 + (tap // 4) * 16, (tap % 4) * 128
                wbuf[c, at, quad, tap] = full[row : row + 16, lanes : lanes + 128]
        whole = wbuf.at[c, at]
        send(whole, whole, wc_s.at[step + 1], wc_r.at[step + 1], core)

    def w_core():
        for step in (0, -1, 1, 2):
            arrived(wbuf.at[1 - c, mod4(x + step)], wc_r.at[step + 1])

    def y_block(owner, half, part):
        return gb.at[owner, pl.ds(2 * half, 2), pl.ds(128 * part, 128)]

    def y_start(part):
        for half in range(2):
            block = y_block(y, half, part)
            send(block, block, gy_s.at[part, 0, half], gy_r.at[part, 0, half], y_right)
            send(block, block, gy_s.at[part, 1, half], gy_r.at[part, 1, half], y_left)

    def y_relay(part):
        for side, step, target in ((0, -1, y_right), (1, 1, y_left)):
            for half in (side, 1 - side):
                block = y_block(mod4(y + step), half, part)
                arrived(block, gy_r.at[part, side, half])
                if half == side:
                    send(block, block, gy_s.at[part, 2, half], gy_r.at[part, 2, half], target)

    def y_far(part):
        for half in range(2):
            arrived(y_block(mod4(y + 2), half, part), gy_r.at[part, 2, half])

    def strips_start(field, tile):
        rows_s[field, 0:32] = tile[96:128]
        rows_s[field, 32:64] = tile[0:32]
        for k, step in enumerate(STRIP_STEPS):
            block = pl.ds(32 * k, 32)
            send(rows_s.at[field, block], rows_r.at[field, block], h_s.at[field, k], h_r.at[field, k], zmove(step))

    def columns_start(field, tile):
        rows_s[field, 64:96] = dot(column_pick[...], tile).astype(BF16)
        for k, step in enumerate(COLUMN_STEPS):
            block = pl.ds(64 + 16 * k, 16)
            send(rows_s.at[field, block], rows_r.at[field, block], h_s.at[field, 2 + k], h_r.at[field, 2 + k], zmove(step))
        corners = [dot(corner_pick[k], tile[:, k * 128 : (k + 1) * 128]) for k in range(4)]
        corners_s[field] = (corners[0] + corners[1] + corners[2] + corners[3]).astype(BF16)
        for k, step in enumerate(CORNER_STEPS):
            block = pl.ds(16 * k, 16)
            send(corners_s.at[field, block], corners_r.at[field, block], h_s.at[field, 4 + k], h_r.at[field, 4 + k], zmove(step))

    tile_row, tile_column = lax.div(z, 4), lax.rem(z, 4)

    def unless(hit):
        return jnp.where(hit, 0.0, 1.0).astype(F32)

    at_top, at_bottom = unless(tile_row == 0), unless(tile_row == 3)
    at_left, at_right = unless(tile_column == 0), unless(tile_column == 3)

    def halo_finish(field):
        for k in range(2):
            arrived(rows_r.at[field, pl.ds(32 * k, 32)], h_r.at[field, k])
        for k in range(2):
            arrived(rows_r.at[field, pl.ds(64 + 16 * k, 16)], h_r.at[field, 2 + k])
        for k in range(4):
            arrived(corners_r.at[field, pl.ds(16 * k, 16)], h_r.at[field, 4 + k])
        above = rows_r[field, 0:32].astype(F32) * at_top
        below = rows_r[field, 32:64].astype(F32) * at_bottom
        row_at = lax.broadcasted_iota(jnp.int32, (64, 128), 0)
        keep = jnp.where((row_at & 8) == 0, at_left, at_right)
        keep = keep * jnp.where((row_at & 7) == 0, at_top, 1.0) * jnp.where((row_at & 7) == 5, at_bottom, 1.0)
        flag = jnp.where(row_at == 6, source, 0.0)
        edges = []
        for k in range(4):
            picks = jnp.concatenate([rows_r[field, 64:96, k * 128 : (k + 1) * 128], corners_r[field]], axis=0)
            edges.append(dot(edge_pick[k, :, 0:96], picks) * keep + flag)
        return jnp.concatenate([above, below, jnp.concatenate(edges, axis=1)], axis=0).astype(BF16)

    loads[0].wait()
    packed = jnp.zeros((112, 128), F32)
    for k in range(4):
        taps = [wv[4 * row + k] if 4 * row + k < 27 else jnp.zeros((16, 32), BF16) for row in range(7)]
        lane_at = lax.broadcasted_iota(jnp.int32, (32, 128), 1) - lax.broadcasted_iota(jnp.int32, (32, 128), 0)
        packed = packed + dot(jnp.concatenate(taps, axis=0), jnp.where(lane_at == 32 * k, 1.0, 0.0).astype(BF16))
    wz[x, 0] = packed.astype(BF16)

    live = jnp.where(count_ref[0] > 0, 1.0, 0.0).astype(F32)
    fresh = jnp.where(starts_ref[0] == 0, 1.0, 0.0).astype(F32)
    source = live * fresh * jnp.where(group > 0, 1.0, 0.0).astype(F32)

    def swap_frames(value):
        value = value.reshape(4, 4, 8, value.shape[1])
        return jnp.concatenate([value[:, k] for k in range(4)], axis=0).reshape(128, value.shape[3])

    loads[1].wait()
    masked = gv[...].astype(F32) * live
    grad_tile = swap_frames(masked).astype(BF16)
    for k in range(4):
        gb[y, k, 0:128] = grad_tile[:, k * 128 : (k + 1) * 128]

    pl.semaphore_wait(barrier, len(partners))
    z_first()
    x_send(0, 0)
    x_send(0, 1)
    y_start(0)

    loads[2].wait()
    loads[3].wait()
    loads[4].wait()
    gain = gainv[...]
    values = xv[...].astype(F32)
    scale = lax.rsqrt(jnp.mean(values * values, axis=-1, keepdims=True) + EPSILON)
    normed = values * scale * gain
    activated = (normed * jax.nn.sigmoid(normed)).astype(BF16)
    swapped = swap_lanes(activated, swap_ref)
    tsend[0:64] = swapped[64:128].astype(BF16)
    act_tile = swap_frames(swapped).astype(BF16)

    def a_rows(part):
        return pl.ds(0, 128) if part == 0 else pl.ds(128, 256)

    def a_start(part, value):
        first = 0 if part == 0 else 128
        for k in range(4):
            amsg[k, first : first + value.shape[0]] = value[:, k * 128 : (k + 1) * 128]
        for d in (1, 2, 3):
            src, dst = amsg.at[mod4(y + d), a_rows(part)], abuf.at[y, a_rows(part)]
            send(src, dst, a_s.at[part, d - 1], a_r.at[part, d - 1], y_peers[d - 1])
        abuf[y, first : first + value.shape[0]] = amsg[y, first : first + value.shape[0]]

    def a_wait(part):
        for d in (1, 2, 3):
            arrived(abuf.at[mod4(y - d), a_rows(part)], a_r.at[part, d - 1])

    a_start(0, act_tile)
    for load in loads[5:]:
        load.wait()
    strips_start(0, act_tile)
    columns_start(0, act_tile)
    z_first_wait()
    z_second()
    for k, side in ((1, 0), (2, 1), (2, 0), (1, 1)):
        x_send(k, side)
    x_pass(0)
    strips_start(1, grad_tile)
    columns_start(1, grad_tile)
    y_relay(0)
    halo = halo_finish(0)
    tsend[64:80] = halo[16:32]
    tsend[80:96] = halo[48:64]
    tsend[96:128] = halo[96:128]
    send(tsend, trecv, t_s.at[0], t_r.at[0], after)
    z_second_wait()
    for k, side in ((3, 0), (4, 1), (4, 0), (3, 1)):
        x_send(k, side)
    x_pass(1)
    x_pass(2)
    w_layout(0)
    arrived(trecv, t_r.at[0])
    a_start(1, jnp.concatenate([halo, (trecv[...].astype(F32) * source).astype(BF16)], axis=0))
    grad_halo = halo_finish(1)
    for k in range(4):
        gb[y, k, 128:256] = grad_halo[:, k * 128 : (k + 1) * 128]
    y_start(1)
    x_pass(3)
    x_pass(4)
    for k in range(5):
        x_arrived(k, 1 - CHUNKS[k][2])
    w_layout(-1)
    w_layout(1)
    y_relay(1)

    def shifted(slabs, centers, edges):
        center = jnp.concatenate([slabs[k : k + 1] for k in centers], axis=0)
        sides = []
        for side in range(2):
            rows = [jnp.broadcast_to(slabs[k + side, i : i + 1], slabs.shape[1:])[None] for k, i in edges]
            sides.append(jnp.concatenate(rows, axis=0))
        at = lax.broadcasted_iota(jnp.int32, center.shape, 1)
        from_left = jnp.where(at == 0, sides[0], pltpu.roll(center, 1, 1))
        from_right = jnp.where(at == 7, sides[1], pltpu.roll(center, 7, 1))
        return from_left, center, from_right

    def own_slab(i, t):
        return 16 + t if i == 0 else 20 + t if i == 5 else (i - 1) * 4 + t

    def carried_slab(i, t):
        return 40 + t if i == 0 else 42 + t if i == 5 else 32 + t * 4 + i - 1

    grad_centers = [own_slab(i, t) for i in range(6) for t in range(4)]
    grad_edges = [(24 + 2 * t, i) for i in range(6) for t in range(4)]
    act_centers = [carried_slab(i, t) if t < 2 else own_slab(i, t - 2) for i in range(6) for t in range(6)]
    act_edges = [(44 + 2 * t, i) if t < 2 else (24 + 2 * (t - 2), i) for i in range(6) for t in range(6)]

    a_wait(0)
    a_wait(1)

    def build_f(pair, carry):
        parts = []
        for k in range(2):
            slabs = abuf[2 * pair + k].astype(F32).reshape(48, 8, 128)
            parts.append(shifted(slabs, act_centers, act_edges))
        rows = pl.ds(pl.multiple_of(16 * pair, 16), 16)
        for e in range(3):
            value = jnp.concatenate([part[e] for part in parts], axis=1).astype(BF16)
            fbuf[e, :, :, rows] = value.reshape(6, 6, 16, 128)
        return carry

    lax.fori_loop(0, 2, build_f, 0)
    for k in range(5):
        x_far(k)
    w_layout(2)

    def build_g(k, carry):
        half, pair = lax.div(k, 2), lax.rem(k, 2)
        parts = []
        for n in range(2):
            message = jnp.concatenate([gb[2 * pair + n, 2 * half + m] for m in range(2)], axis=1)
            parts.append(shifted(message.astype(F32).reshape(32, 8, 256), grad_centers, grad_edges))
        rows = pl.ds(pl.multiple_of(16 * pair, 16), 16)
        for e in range(3):
            value = jnp.concatenate([part[e] for part in parts], axis=1).astype(BF16)
            for m in range(2):
                bbuf[2 * half + m, e, :, :, rows] = value[:, :, m * 128 : (m + 1) * 128].reshape(6, 4, 16, 128)
        return carry

    def taps_of(r, tap):
        return jnp.concatenate([wbuf[k, i, r, tap] for i in range(4) for k in range(2)], axis=0)

    def forward(pair):
        acc_f[...] = jnp.zeros_like(acc_f)

        def frame_tap(a, carry):
            windows, taps = [], []
            for b in range(3):
                for e in range(3):
                    windows.append(fbuf[e, b : b + 4, pl.ds(a, 4)].reshape(512, 128))
                    tap = a * 9 + b * 3 + e
                    taps.append(jnp.concatenate([taps_of(2 * pair + k, tap) for k in range(2)], axis=1))
            acc_f[...] += dot(jnp.concatenate(windows, axis=1), jnp.concatenate(taps, axis=0))
            return carry

        lax.fori_loop(0, 3, frame_tap, 0)
        total = acc_f[...].reshape(16, 32, 256)
        for other in range(4):
            psend[pair, other] = total[:, other * 8 : other * 8 + 8].reshape(128, 256).astype(BF16)
        for d in (1, 2, 3):
            send(psend.at[pair, mod4(y + d)], precv.at[pair, d - 1], p_s.at[pair, d - 1], p_r.at[pair, d - 1], y_peers[d - 1])

    def backward(pair):
        def row_tap(b, carry):
            windows, taps = [], []
            for e in range(3):
                for r in (2 * pair, 2 * pair + 1):
                    windows.append(bbuf[r, 2 - e, pl.ds(2 - b, 4)].reshape(512, 128))
                    taps.append(jnp.concatenate([taps_of(r, a * 9 + b * 3 + e) for a in range(3)], axis=0))
            acc_b[...] += lax.dot_general(
                jnp.concatenate(windows, axis=1),
                jnp.concatenate(taps, axis=1),
                (((1,), (1,)), ((), ())),
                preferred_element_type=F32,
            )
            return carry

        lax.fori_loop(0, 3, row_tap, 0)

    def reduce(pair):
        total = psend[pair, y].astype(F32)
        for d in (1, 2, 3):
            arrived(precv.at[pair, d - 1], p_r.at[pair, d - 1])
            total = total + precv[pair, d - 1].astype(F32)
        mix[2 * pair] = total[:, 0:128]
        mix[2 * pair + 1] = total[:, 128:256]

    y_far(0)
    y_far(1)
    lax.fori_loop(0, 4, build_g, 0)
    acc_b[...] = jnp.zeros_like(acc_b)
    w_core()
    forward(0)
    forward(1)
    backward(0)
    backward(1)
    taps = acc_b[...].reshape(4, 4, 32, 384)
    spread = []
    for u in range(6):
        terms = [taps[:, u - a, :, a * 128 : (a + 1) * 128] for a in range(3) if 0 <= u - a < 4]
        spread.append(sum(terms[1:], terms[0]))
    for other in range(4):
        slots = [part[:, other * 8 : other * 8 + 8] for part in spread]
        bsend[other] = jnp.stack(slots[2:], axis=1).reshape(128, 128).astype(BF16)
        flag = gb[other, 0, 192:208].astype(F32)[6:7]
        dsend[other] = (jnp.stack(slots[:2], axis=1).reshape(64, 128) * flag).astype(BF16)
    for d in (1, 2, 3):
        send(bsend.at[mod4(y + d)], brecv.at[y], b_s.at[d - 1], b_r.at[d - 1], y_peers[d - 1])
    for k in range(4):
        send(dsend.at[k], drecv.at[y], d_s.at[k], d_r.at[y], head_targets[k])
    brecv[y] = bsend[y]
    reduce(0)
    reduce(1)
    mixed = jnp.concatenate([mix[k] for k in range(4)], axis=1)
    out_ref[...] = ((values + swap_frames(mixed)) * live).astype(BF16)
    for copy in started[:-7]:
        copy.wait_send()
    for d in (1, 2, 3):
        arrived(brecv.at[mod4(y - d)], b_r.at[d - 1])
    for k in range(4):
        arrived(drecv.at[k], d_r.at[k])
    own = jnp.concatenate([brecv[k] for k in range(4)], axis=1).astype(F32).reshape(4, 4, 8, 512)
    heads = jnp.concatenate([drecv[k] for k in range(4)], axis=1).astype(F32).reshape(4, 2, 8, 512)
    upstream = swap_lanes(own.reshape(128, 512).astype(BF16), swap_ref).reshape(4, 4, 8, 512)
    tails = swap_lanes(heads.reshape(64, 512).astype(BF16), swap_ref).reshape(4, 2, 8, 512)
    upstream = jnp.concatenate(
        [upstream[:, 0], upstream[:, 1], upstream[:, 2] + tails[:, 0], upstream[:, 3] + tails[:, 1]], axis=0
    ).reshape(128, 512)
    sigma = jax.nn.sigmoid(normed)
    through = upstream * sigma * (1.0 + normed * (1.0 - sigma)) * gain
    cubed = scale * scale * scale
    through_mean = jnp.mean(values * through, axis=-1, keepdims=True)
    gradient = masked + scale * through - values * cubed * through_mean
    grad_ref[...] = (gradient * live).astype(BF16)
    for copy in started[-7:]:
        copy.wait_send()


def pin(value):
    return pltpu.with_memory_space_constraint(value, pltpu.HBM)


def per_device(block_input_frames, norm_gain, kernel, output_gradient, group_count, clip_starts):
    shape = block_input_frames.shape
    tables = [jnp.asarray(table(), BF16) for table in (swap_table, column_table, corner_table, edge_table)]
    vmem, smem, hbm = [pl.BlockSpec(memory_space=space) for space in (pltpu.VMEM, pltpu.SMEM, pltpu.HBM)]
    dma = pltpu.SemaphoreType.DMA
    block_out, input_grad = pl.pallas_call(
        body,
        out_shape=[jax.ShapeDtypeStruct((128, 512), BF16)] * 2,
        in_specs=[hbm] * 4 + [smem] * 2 + [hbm] * 4,
        out_specs=[vmem] * 2,
        scratch_shapes=[
            pltpu.VMEM((128, 512), BF16),
            pltpu.VMEM((1, 512), F32),
            pltpu.VMEM((27, 16, 32), BF16),
            pltpu.VMEM((128, 512), BF16),
            *[pltpu.VMEM(table.shape, BF16) for table in tables],
            pltpu.VMEM((4, 16, 112, 128), BF16),
            pltpu.VMEM((2, 4, 4, 27, 16, 128), BF16),
            pltpu.VMEM((128, 512), BF16),
            pltpu.VMEM((128, 512), BF16),
            pltpu.VMEM((2, 96, 512), BF16),
            pltpu.VMEM((2, 96, 512), BF16),
            pltpu.VMEM((2, 64, 128), BF16),
            pltpu.VMEM((2, 64, 128), BF16),
            pltpu.VMEM((4, 384, 128), BF16),
            pltpu.VMEM((4, 384, 128), BF16),
            pltpu.VMEM((4, 4, 256, 128), BF16),
            pltpu.VMEM((3, 6, 6, 32, 128), BF16),
            pltpu.VMEM((4, 3, 6, 4, 32, 128), BF16),
            pltpu.VMEM((512, 256), F32),
            pltpu.VMEM((512, 384), F32),
            pltpu.VMEM((2, 4, 128, 256), BF16),
            pltpu.VMEM((2, 3, 128, 256), BF16),
            pltpu.VMEM((4, 128, 128), BF16),
            pltpu.VMEM((4, 128, 128), BF16),
            pltpu.VMEM((4, 64, 128), BF16),
            pltpu.VMEM((4, 64, 128), BF16),
            pltpu.VMEM((4, 128, 128), F32),
            dma((8,)),
            dma((8,)), dma((8,)),
            dma((1,)), dma((1,)),
            dma((2, 8)), dma((2, 8)),
            dma((2, 3)), dma((2, 3)),
            dma((2, 3, 2)), dma((2, 3, 2)),
            dma((2, 5)), dma((2, 5)),
            dma((5,)), dma((5,)),
            dma((4,)), dma((4,)),
            dma((2, 3)), dma((2, 3)),
            dma((3,)), dma((3,)),
            dma((4,)), dma((4,)),
        ],
        compiler_params=pltpu.CompilerParams(
            collective_id=0, has_side_effects=True, vmem_limit_bytes=40 * 1024 * 1024
        ),
        cost_estimate=pl.CostEstimate(flops=7_200_000_000, bytes_accessed=20_000_000, transcendentals=200_000),
    )(
        pin(block_input_frames.reshape(128, 512)),
        pin(norm_gain.reshape(1, 512)),
        pin(kernel.reshape(27, 16, 32)),
        pin(output_gradient.reshape(128, 512)),
        group_count,
        clip_starts,
        *[pin(table) for table in tables],
    )
    return block_out.reshape(shape), input_grad.reshape(shape)


def solution(mesh):
    frames = P("group", None, "tile", None, None, None)
    return jax.shard_map(
        per_device,
        mesh=mesh,
        in_specs=(frames, P(), P(None, None, None, "group", "tile"), frames, P("group"), P("group")),
        out_specs=(frames, frames),
        check_vma=False,
    )
```

time: 289 us -> 65 us (0.22)
  the two profiles are of different devices: /device:TPU:68 before, /device:TPU:1 now
where the time goes in v1:
time: 65 us; the launch traced here: 64.5 us
  Pallas kernels  61.3 us (94%)
  between operations  1.93 us (3%)
  local copies, waits for them, and re-layouts  1.31 us (2%)
    pallas_call x1, Pallas kernels, per_device(): pl.pallas_call(body, out_shape=[jax.ShapeDtypeStruct((128, 512), BF16)] *...  61.3 us
    unnamed x2, local copies, waits for them, and re-layouts  1.31 us

profile of v1, /device:TPU:1, one launch (start us, length us, event | category | flops | bytes accessed | tf_op | source)
XLA Modules:
  0.0 64.5 jit_solution(15373048513146094504)
XLA Ops:
  1.9 61.3 %shard_map.113 = (bf16[128,512]{1,0:T(8,128)(2,1)S(1)}, bf16[128,512]{1,0:T(8,128)(2,1)S(1)}) custom-call(bf16[128,512]{1,0:T(8,128)(2,1)} %bitcast.12, f32[1,512]{1,0:T(1,128)} %bitcast.15, bf16[27,16,32]{2,1,0:T(8,128)(2,1)} %bitcast.14, bf16[128,512]{1,0:T(8,128)(2,1)} %bitcast.13, s32[1]{0:T(128)S(6)} %copy.16.count_ref, s32[1]{0:T(128)S(6)} %copy.17.starts_ref, ...), custom_call_target="tpu_custom_call" | custom-call | flops 7200000000 | bytes 20000000 | tf_op jit(solution)/shard_map/pallas_call | solution.py:512
  63.2 0.7 %copy.18 = bf16[1,4,1,4,8,512]{5,4,3,2,1,0:T(8,128)(2,1)} copy(bf16[1,4,1,4,8,512]{5,4,3,2,1,0:T(8,128)(2,1)S(1)} %bitcast.11) | data formatting | bytes 262144
  63.9 0.7 %copy.19 = bf16[1,4,1,4,8,512]{5,4,3,2,1,0:T(8,128)(2,1)} copy(bf16[1,4,1,4,8,512]{5,4,3,2,1,0:T(8,128)(2,1)S(1)} %bitcast.10) | data formatting | bytes 262144

commit v2 on v1

--- a/solution.py
+++ b/solution.py
@@ -68,7 +68,7 @@
     out_ref, grad_ref,
     xv, gainv, wv, gv, swap_ref, column_pick, corner_pick, edge_pick,
     wz, wbuf, tsend, trecv, rows_s, rows_r, corners_s, corners_r, amsg, abuf, gb, fbuf, bbuf,
-    acc_f, acc_b, psend, precv, bsend, brecv, dsend, drecv, mix,
+    acc_f, acc_b, psend, precv, bsend, brecv, dsend, drecv,
     in_s, z_s, z_r, t_s, t_r, h_s, h_r, a_s, a_r, gy_s, gy_r,
     wx_s, wx_r, wf_s, wf_r, wc_s, wc_r, p_s, p_r, b_s, b_r, d_s, d_r,
 ):
@@ -384,9 +384,6 @@
         return carry
 
     lax.fori_loop(0, 2, build_f, 0)
-    for k in range(5):
-        x_far(k)
-    w_layout(2)
 
     def build_g(k, carry):
         half, pair = lax.div(k, 2), lax.rem(k, 2)
@@ -404,7 +401,7 @@
     def taps_of(r, tap):
         return jnp.concatenate([wbuf[k, i, r, tap] for i in range(4) for k in range(2)], axis=0)
 
-    def forward(pair):
+    def forward():
         acc_f[...] = jnp.zeros_like(acc_f)
 
         def frame_tap(a, carry):
@@ -413,24 +410,26 @@
                 for e in range(3):
                     windows.append(fbuf[e, b : b + 4, pl.ds(a, 4)].reshape(512, 128))
                     tap = a * 9 + b * 3 + e
-                    taps.append(jnp.concatenate([taps_of(2 * pair + k, tap) for k in range(2)], axis=1))
+                    taps.append(jnp.concatenate([taps_of(quad, tap) for quad in range(4)], axis=1))
             acc_f[...] += dot(jnp.concatenate(windows, axis=1), jnp.concatenate(taps, axis=0))
             return carry
 
         lax.fori_loop(0, 3, frame_tap, 0)
-        total = acc_f[...].reshape(16, 32, 256)
+        total = acc_f[...].reshape(16, 32, 512)
         for other in range(4):
-            psend[pair, other] = total[:, other * 8 : other * 8 + 8].reshape(128, 256).astype(BF16)
+            psend[other] = total[:, other * 8 : other * 8 + 8].reshape(128, 512).astype(BF16)
         for d in (1, 2, 3):
-            send(psend.at[pair, mod4(y + d)], precv.at[pair, d - 1], p_s.at[pair, d - 1], p_r.at[pair, d - 1], y_peers[d - 1])
-
-    def backward(pair):
+            send(psend.at[mod4(y + d)], precv.at[d - 1], p_s.at[d - 1], p_r.at[d - 1], y_peers[d - 1])
+
+    def backward():
+        acc_b[...] = jnp.zeros_like(acc_b)
+
         def row_tap(b, carry):
             windows, taps = [], []
             for e in range(3):
-                for r in (2 * pair, 2 * pair + 1):
-                    windows.append(bbuf[r, 2 - e, pl.ds(2 - b, 4)].reshape(512, 128))
-                    taps.append(jnp.concatenate([taps_of(r, a * 9 + b * 3 + e) for a in range(3)], axis=0))
+                for quad in range(4):
+                    windows.append(bbuf[quad, 2 - e, pl.ds(2 - b, 4)].reshape(512, 128))
+                    taps.append(jnp.concatenate([taps_of(quad, a * 9 + b * 3 + e) for a in range(3)], axis=0))
             acc_b[...] += lax.dot_general(
                 jnp.concatenate(windows, axis=1),
                 jnp.concatenate(taps, axis=1),
@@ -441,23 +440,17 @@
 
         lax.fori_loop(0, 3, row_tap, 0)
 
-    def reduce(pair):
-        total = psend[pair, y].astype(F32)
-        for d in (1, 2, 3):
-            arrived(precv.at[pair, d - 1], p_r.at[pair, d - 1])
-            total = total + precv[pair, d - 1].astype(F32)
-        mix[2 * pair] = total[:, 0:128]
-        mix[2 * pair + 1] = total[:, 128:256]
-
+    sigma = jax.nn.sigmoid(normed)
+    slope = sigma * (1.0 + normed * (1.0 - sigma)) * gain
     y_far(0)
     y_far(1)
     lax.fori_loop(0, 4, build_g, 0)
-    acc_b[...] = jnp.zeros_like(acc_b)
+    for k in range(5):
+        x_far(k)
+    w_layout(2)
     w_core()
-    forward(0)
-    forward(1)
-    backward(0)
-    backward(1)
+    forward()
+    backward()
     taps = acc_b[...].reshape(4, 4, 32, 384)
     spread = []
     for u in range(6):
@@ -473,9 +466,10 @@
     for k in range(4):
         send(dsend.at[k], drecv.at[y], d_s.at[k], d_r.at[y], head_targets[k])
     brecv[y] = bsend[y]
-    reduce(0)
-    reduce(1)
-    mixed = jnp.concatenate([mix[k] for k in range(4)], axis=1)
+    mixed = psend[y].astype(F32)
+    for d in (1, 2, 3):
+        arrived(precv.at[d - 1], p_r.at[d - 1])
+        mixed = mixed + precv[d - 1].astype(F32)
     out_ref[...] = ((values + swap_frames(mixed)) * live).astype(BF16)
     for copy in started[:-7]:
         copy.wait_send()
@@ -490,8 +484,7 @@
     upstream = jnp.concatenate(
         [upstream[:, 0], upstream[:, 1], upstream[:, 2] + tails[:, 0], upstream[:, 3] + tails[:, 1]], axis=0
     ).reshape(128, 512)
-    sigma = jax.nn.sigmoid(normed)
-    through = upstream * sigma * (1.0 + normed * (1.0 - sigma)) * gain
+    through = upstream * slope
     cubed = scale * scale * scale
     through_mean = jnp.mean(values * through, axis=-1, keepdims=True)
     gradient = masked + scale * through - values * cubed * through_mean
@@ -533,15 +526,14 @@
             pltpu.VMEM((4, 4, 256, 128), BF16),
             pltpu.VMEM((3, 6, 6, 32, 128), BF16),
             pltpu.VMEM((4, 3, 6, 4, 32, 128), BF16),
-            pltpu.VMEM((512, 256), F32),
+            pltpu.VMEM((512, 512), F32),
             pltpu.VMEM((512, 384), F32),
-            pltpu.VMEM((2, 4, 128, 256), BF16),
-            pltpu.VMEM((2, 3, 128, 256), BF16),
+            pltpu.VMEM((4, 128, 512), BF16),
+            pltpu.VMEM((3, 128, 512), BF16),
             pltpu.VMEM((4, 128, 128), BF16),
             pltpu.VMEM((4, 128, 128), BF16),
             pltpu.VMEM((4, 64, 128), BF16),
             pltpu.VMEM((4, 64, 128), BF16),
-            pltpu.VMEM((4, 128, 128), F32),
             dma((8,)),
             dma((8,)), dma((8,)),
             dma((1,)), dma((1,)),
@@ -551,7 +543,7 @@
             dma((2, 5)), dma((2, 5)),
             dma((5,)), dma((5,)),
             dma((4,)), dma((4,)),
-            dma((2, 3)), dma((2, 3)),
+            dma((3,)), dma((3,)),
             dma((3,)), dma((3,)),
             dma((4,)), dma((4,)),
         ],

time: 65 us -> 66.7 us (1.026)
  Pallas kernels: 61.3 us -> 63.3 us
    pallas_call x1, Pallas kernels: 61.3 us -> 63.3 us  [per_device(): pl.pallas_call(body, out_shape=[jax.ShapeDtypeStruct((128, 512), BF16)] *...]
where the time goes in v2:
time: 66.7 us; the launch traced here: 66.6 us
  Pallas kernels  63.3 us (95%)
  between operations  1.93 us (3%)
  local copies, waits for them, and re-layouts  1.31 us (2%)
    pallas_call x1, Pallas kernels, per_device(): pl.pallas_call(body, out_shape=[jax.ShapeDtypeStruct((128, 512), BF16)] *...  63.3 us

profile of v2, /device:TPU:1, one launch (start us, length us, event | category | flops | bytes accessed | tf_op | source)
XLA Modules:
  0.0 66.6 jit_solution(9398268910633428558)
XLA Ops:
  1.9 63.3 %shard_map.113 = (bf16[128,512]{1,0:T(8,128)(2,1)S(1)}, bf16[128,512]{1,0:T(8,128)(2,1)S(1)}) custom-call(bf16[128,512]{1,0:T(8,128)(2,1)} %bitcast.12, f32[1,512]{1,0:T(1,128)} %bitcast.15, bf16[27,16,32]{2,1,0:T(8,128)(2,1)} %bitcast.14, bf16[128,512]{1,0:T(8,128)(2,1)} %bitcast.13, s32[1]{0:T(128)S(6)} %copy.16.count_ref, s32[1]{0:T(128)S(6)} %copy.17.starts_ref, ...), custom_call_target="tpu_custom_call" | custom-call | flops 7200000000 | bytes 20000000 | tf_op jit(solution)/shard_map/pallas_call | solution.py:505
  65.3 0.7 copy.18
  65.9 0.7 copy.19

commit v3 on v2

--- a/solution.py
+++ b/solution.py
@@ -318,9 +318,9 @@
     z_second()
     for k, side in ((1, 0), (2, 1), (2, 0), (1, 1)):
         x_send(k, side)
-    x_pass(0)
     strips_start(1, grad_tile)
     columns_start(1, grad_tile)
+    x_pass(0)
     y_relay(0)
     halo = halo_finish(0)
     tsend[64:80] = halo[16:32]
@@ -330,22 +330,22 @@
     z_second_wait()
     for k, side in ((3, 0), (4, 1), (4, 0), (3, 1)):
         x_send(k, side)
+    grad_halo = halo_finish(1)
+    for k in range(4):
+        gb[y, k, 128:256] = grad_halo[:, k * 128 : (k + 1) * 128]
+    y_start(1)
     x_pass(1)
     x_pass(2)
     w_layout(0)
     arrived(trecv, t_r.at[0])
     a_start(1, jnp.concatenate([halo, (trecv[...].astype(F32) * source).astype(BF16)], axis=0))
-    grad_halo = halo_finish(1)
-    for k in range(4):
-        gb[y, k, 128:256] = grad_halo[:, k * 128 : (k + 1) * 128]
-    y_start(1)
     x_pass(3)
     x_pass(4)
+    y_relay(1)
     for k in range(5):
         x_arrived(k, 1 - CHUNKS[k][2])
     w_layout(-1)
     w_layout(1)
-    y_relay(1)
 
     def shifted(slabs, centers, edges):
         center = jnp.concatenate([slabs[k : k + 1] for k in centers], axis=0)
@@ -442,12 +442,12 @@
 
     sigma = jax.nn.sigmoid(normed)
     slope = sigma * (1.0 + normed * (1.0 - sigma)) * gain
+    for k in range(5):
+        x_far(k)
+    w_layout(2)
     y_far(0)
     y_far(1)
     lax.fori_loop(0, 4, build_g, 0)
-    for k in range(5):
-        x_far(k)
-    w_layout(2)
     w_core()
     forward()
     backward()

time: 66.7 us -> 65.9 us (0.988)
  Pallas kernels: 63.3 us -> 62.5 us
    pallas_call x1, Pallas kernels: 63.3 us -> 62.5 us  [per_device(): pl.pallas_call(body, out_shape=[jax.ShapeDtypeStruct((128, 512), BF16)] *...]
where the time goes in v3:
time: 65.9 us; the launch traced here: 65.8 us
  Pallas kernels  62.5 us (95%)
  between operations  1.93 us (3%)
  local copies, waits for them, and re-layouts  1.31 us (2%)
    pallas_call x1, Pallas kernels, per_device(): pl.pallas_call(body, out_shape=[jax.ShapeDtypeStruct((128, 512), BF16)] *...  62.5 us

profile of v3, /device:TPU:1, one launch (start us, length us, event | category | flops | bytes accessed | tf_op | source)
XLA Modules:
  0.0 65.8 jit_solution(13438584399603647386)
XLA Ops:
  1.9 62.5 %shard_map.113 = (bf16[128,512]{1,0:T(8,128)(2,1)S(1)}, bf16[128,512]{1,0:T(8,128)(2,1)S(1)}) custom-call(bf16[128,512]{1,0:T(8,128)(2,1)} %bitcast.12, f32[1,512]{1,0:T(1,128)} %bitcast.15, bf16[27,16,32]{2,1,0:T(8,128)(2,1)} %bitcast.14, bf16[128,512]{1,0:T(8,128)(2,1)} %bitcast.13, s32[1]{0:T(128)S(6)} %copy.16.count_ref, s32[1]{0:T(128)S(6)} %copy.17.starts_ref, ...), custom_call_target="tpu_custom_call" | custom-call | flops 7200000000 | bytes 20000000 | tf_op jit(solution)/shard_map/pallas_call | solution.py:505
  64.5 0.7 %copy.18 = bf16[1,4,1,4,8,512]{5,4,3,2,1,0:T(8,128)(2,1)} copy(bf16[1,4,1,4,8,512]{5,4,3,2,1,0:T(8,128)(2,1)S(1)} %bitcast.11) | data formatting | bytes 262144
  65.1 0.7 copy.19

commit v4 on v3

--- a/solution.py
+++ b/solution.py
@@ -401,7 +401,7 @@
     def taps_of(r, tap):
         return jnp.concatenate([wbuf[k, i, r, tap] for i in range(4) for k in range(2)], axis=0)
 
-    def forward():
+    def forward(pair):
         acc_f[...] = jnp.zeros_like(acc_f)
 
         def frame_tap(a, carry):
@@ -410,16 +410,17 @@
                 for e in range(3):
                     windows.append(fbuf[e, b : b + 4, pl.ds(a, 4)].reshape(512, 128))
                     tap = a * 9 + b * 3 + e
-                    taps.append(jnp.concatenate([taps_of(quad, tap) for quad in range(4)], axis=1))
+                    taps.append(jnp.concatenate([taps_of(2 * pair + k, tap) for k in range(2)], axis=1))
             acc_f[...] += dot(jnp.concatenate(windows, axis=1), jnp.concatenate(taps, axis=0))
             return carry
 
         lax.fori_loop(0, 3, frame_tap, 0)
-        total = acc_f[...].reshape(16, 32, 512)
+        total = acc_f[...].reshape(16, 32, 256)
         for other in range(4):
-            psend[other] = total[:, other * 8 : other * 8 + 8].reshape(128, 512).astype(BF16)
+            psend[pair, other] = total[:, other * 8 : other * 8 + 8].reshape(128, 256).astype(BF16)
         for d in (1, 2, 3):
-            send(psend.at[mod4(y + d)], precv.at[d - 1], p_s.at[d - 1], p_r.at[d - 1], y_peers[d - 1])
+            src, dst = psend.at[pair, mod4(y + d)], precv.at[pair, d - 1]
+            send(src, dst, p_s.at[pair, d - 1], p_r.at[pair, d - 1], y_peers[d - 1])
 
     def backward():
         acc_b[...] = jnp.zeros_like(acc_b)
@@ -449,7 +450,8 @@
     y_far(1)
     lax.fori_loop(0, 4, build_g, 0)
     w_core()
-    forward()
+    forward(0)
+    forward(1)
     backward()
     taps = acc_b[...].reshape(4, 4, 32, 384)
     spread = []
@@ -466,10 +468,14 @@
     for k in range(4):
         send(dsend.at[k], drecv.at[y], d_s.at[k], d_r.at[y], head_targets[k])
     brecv[y] = bsend[y]
-    mixed = psend[y].astype(F32)
-    for d in (1, 2, 3):
-        arrived(precv.at[d - 1], p_r.at[d - 1])
-        mixed = mixed + precv[d - 1].astype(F32)
+    halves = []
+    for pair in range(2):
+        total = psend[pair, y].astype(F32)
+        for d in (1, 2, 3):
+            arrived(precv.at[pair, d - 1], p_r.at[pair, d - 1])
+            total = total + precv[pair, d - 1].astype(F32)
+        halves.append(total)
+    mixed = jnp.concatenate(halves, axis=1)
     out_ref[...] = ((values + swap_frames(mixed)) * live).astype(BF16)
     for copy in started[:-7]:
         copy.wait_send()
@@ -526,10 +532,10 @@
             pltpu.VMEM((4, 4, 256, 128), BF16),
             pltpu.VMEM((3, 6, 6, 32, 128), BF16),
             pltpu.VMEM((4, 3, 6, 4, 32, 128), BF16),
-            pltpu.VMEM((512, 512), F32),
+            pltpu.VMEM((512, 256), F32),
             pltpu.VMEM((512, 384), F32),
-            pltpu.VMEM((4, 128, 512), BF16),
-            pltpu.VMEM((3, 128, 512), BF16),
+            pltpu.VMEM((2, 4, 128, 256), BF16),
+            pltpu.VMEM((2, 3, 128, 256), BF16),
             pltpu.VMEM((4, 128, 128), BF16),
             pltpu.VMEM((4, 128, 128), BF16),
             pltpu.VMEM((4, 64, 128), BF16),
@@ -543,7 +549,7 @@
             dma((2, 5)), dma((2, 5)),
             dma((5,)), dma((5,)),
             dma((4,)), dma((4,)),
-            dma((3,)), dma((3,)),
+            dma((2, 3)), dma((2, 3)),
             dma((3,)), dma((3,)),
             dma((4,)), dma((4,)),
         ],

time: 65.9 us -> 64.9 us (0.985)
  Pallas kernels: 62.5 us -> 61.5 us
    pallas_call x1, Pallas kernels: 62.5 us -> 61.5 us  [per_device(): pl.pallas_call(body, out_shape=[jax.ShapeDtypeStruct((128, 512), BF16)] *...]
where the time goes in v4:
time: 64.9 us; the launch traced here: 64.8 us
  Pallas kernels  61.5 us (95%)
  between operations  1.93 us (3%)
  local copies, waits for them, and re-layouts  1.31 us (2%)
    pallas_call x1, Pallas kernels, per_device(): pl.pallas_call(body, out_shape=[jax.ShapeDtypeStruct((128, 512), BF16)] *...  61.5 us
    unnamed x2, local copies, waits for them, and re-layouts  1.31 us

profile of v4, /device:TPU:1, one launch (start us, length us, event | category | flops | bytes accessed | tf_op | source)
XLA Modules:
  0.0 64.8 jit_solution(5885941928894411838)
XLA Ops:
  1.9 61.5 %shard_map.113 = (bf16[128,512]{1,0:T(8,128)(2,1)S(1)}, bf16[128,512]{1,0:T(8,128)(2,1)S(1)}) custom-call(bf16[128,512]{1,0:T(8,128)(2,1)} %bitcast.12, f32[1,512]{1,0:T(1,128)} %bitcast.15, bf16[27,16,32]{2,1,0:T(8,128)(2,1)} %bitcast.14, bf16[128,512]{1,0:T(8,128)(2,1)} %bitcast.13, s32[1]{0:T(128)S(6)} %copy.16.count_ref, s32[1]{0:T(128)S(6)} %copy.17.starts_ref, ...), custom_call_target="tpu_custom_call" | custom-call | flops 7200000000 | bytes 20000000 | tf_op jit(solution)/shard_map/pallas_call | solution.py:511
  63.5 0.7 %copy.18 = bf16[1,4,1,4,8,512]{5,4,3,2,1,0:T(8,128)(2,1)} copy(bf16[1,4,1,4,8,512]{5,4,3,2,1,0:T(8,128)(2,1)S(1)} %bitcast.11) | data formatting | bytes 262144
  64.1 0.7 %copy.19 = bf16[1,4,1,4,8,512]{5,4,3,2,1,0:T(8,128)(2,1)} copy(bf16[1,4,1,4,8,512]{5,4,3,2,1,0:T(8,128)(2,1)S(1)} %bitcast.10) | data formatting | bytes 262144

commit v5 on v4

--- a/solution.py
+++ b/solution.py
@@ -50,8 +50,8 @@
     return table
 
 
-SHARDS = (0, -1, 7, -4, -7, 4, 1, -2, 6, -5, -8, 3, -3, -6, 5, 2)
-CHUNKS = ((0, 1, 0), (1, 3, 0), (4, 3, 1), (7, 5, 0), (12, 4, 1))
+SHARDS = (0, -1, 6, -6, 1, -2, 5, -7, 7, -5, 2, -3, 4, -8, -4, 3)
+CHUNKS = ((0, 1, 0), (1, 2, 0), (3, 2, 1), (5, 3, 0), (8, 3, 1), (11, 3, 0), (14, 2, 1))
 STRIP_STEPS, COLUMN_STEPS, CORNER_STEPS = (4, -4), (1, -1), (5, 3, -3, -5)
 
 
@@ -108,7 +108,7 @@
 
     barrier = pltpu.get_barrier_semaphore()
     partners = [core, x_right, x_left, *y_peers, after, before, *head_sources]
-    partners += [zmove(step) for step in STRIP_STEPS + COLUMN_STEPS + CORNER_STEPS + (7, -7)]
+    partners += [zmove(step) for step in STRIP_STEPS + COLUMN_STEPS + CORNER_STEPS + (6, -6)]
     for partner in partners:
         pl.semaphore_signal(barrier, inc=1, device_id=partner, device_id_type=MESH)
 
@@ -128,20 +128,28 @@
         remote(dst, dst, sem, sem, core).wait_recv()
 
     def z_first():
-        for k, step in enumerate(SHARDS[1:7]):
+        for k, step in enumerate(SHARDS[1:5]):
             send(wz.at[x, 0], wz.at[x, 1 + k], z_s.at[k], z_r.at[k], zmove(-step))
 
     def z_first_wait():
-        for k in range(6):
+        for k in range(4):
             arrived(wz.at[x, 1 + k], z_r.at[k])
 
     def z_second():
-        send(wz.at[x, pl.ds(1, 5)], wz.at[x, pl.ds(7, 5)], z_s.at[6], z_r.at[6], zmove(1))
-        send(wz.at[x, pl.ds(3, 4)], wz.at[x, pl.ds(12, 4)], z_s.at[7], z_r.at[7], zmove(-1))
+        send(wz.at[x, pl.ds(1, 3)], wz.at[x, pl.ds(5, 3)], z_s.at[4], z_r.at[4], zmove(1))
+        send(wz.at[x, pl.ds(2, 3)], wz.at[x, pl.ds(8, 3)], z_s.at[5], z_r.at[5], zmove(-1))
 
     def z_second_wait():
-        arrived(wz.at[x, pl.ds(7, 5)], z_r.at[6])
-        arrived(wz.at[x, pl.ds(12, 4)], z_r.at[7])
+        arrived(wz.at[x, pl.ds(5, 3)], z_r.at[4])
+        arrived(wz.at[x, pl.ds(8, 3)], z_r.at[5])
+
+    def z_third():
+        send(wz.at[x, pl.ds(5, 3)], wz.at[x, pl.ds(11, 3)], z_s.at[6], z_r.at[6], zmove(1))
+        send(wz.at[x, pl.ds(9, 2)], wz.at[x, pl.ds(14, 2)], z_s.at[7], z_r.at[7], zmove(-1))
+
+    def z_third_wait():
+        arrived(wz.at[x, pl.ds(11, 3)], z_r.at[6])
+        arrived(wz.at[x, pl.ds(14, 2)], z_r.at[7])
 
     def x_block(step, k):
         return wz.at[mod4(x + step), pl.ds(CHUNKS[k][0], CHUNKS[k][1])]
@@ -328,21 +336,27 @@
     tsend[96:128] = halo[96:128]
     send(tsend, trecv, t_s.at[0], t_r.at[0], after)
     z_second_wait()
+    z_third()
     for k, side in ((3, 0), (4, 1), (4, 0), (3, 1)):
         x_send(k, side)
+    x_pass(1)
+    x_pass(2)
     grad_halo = halo_finish(1)
     for k in range(4):
         gb[y, k, 128:256] = grad_halo[:, k * 128 : (k + 1) * 128]
     y_start(1)
-    x_pass(1)
-    x_pass(2)
+    z_third_wait()
+    for k, side in ((5, 0), (6, 1), (6, 0), (5, 1)):
+        x_send(k, side)
+    x_pass(3)
+    x_pass(4)
     w_layout(0)
     arrived(trecv, t_r.at[0])
     a_start(1, jnp.concatenate([halo, (trecv[...].astype(F32) * source).astype(BF16)], axis=0))
-    x_pass(3)
-    x_pass(4)
+    x_pass(5)
+    x_pass(6)
     y_relay(1)
-    for k in range(5):
+    for k in range(7):
         x_arrived(k, 1 - CHUNKS[k][2])
     w_layout(-1)
     w_layout(1)
@@ -443,7 +457,7 @@
 
     sigma = jax.nn.sigmoid(normed)
     slope = sigma * (1.0 + normed * (1.0 - sigma)) * gain
-    for k in range(5):
+    for k in range(7):
         x_far(k)
     w_layout(2)
     y_far(0)
@@ -546,8 +560,8 @@
             dma((2, 8)), dma((2, 8)),
             dma((2, 3)), dma((2, 3)),
             dma((2, 3, 2)), dma((2, 3, 2)),
-            dma((2, 5)), dma((2, 5)),
-            dma((5,)), dma((5,)),
+            dma((2, 7)), dma((2, 7)),
+            dma((7,)), dma((7,)),
             dma((4,)), dma((4,)),
             dma((2, 3)), dma((2, 3)),
             dma((3,)), dma((3,)),

time: 64.9 us -> 63.3 us (0.975)
  Pallas kernels: 61.5 us -> 59.9 us
    pallas_call x1, Pallas kernels: 61.5 us -> 59.9 us  [per_device(): pl.pallas_call(body, out_shape=[jax.ShapeDtypeStruct((128, 512), BF16)] *...]
where the time goes in v5:
time: 63.3 us; the launch traced here: 63.2 us
  Pallas kernels  59.9 us (95%)
  between operations  1.93 us (3%)
  local copies, waits for them, and re-layouts  1.31 us (2%)
    pallas_call x1, Pallas kernels, per_device(): pl.pallas_call(body, out_shape=[jax.ShapeDtypeStruct((128, 512), BF16)] *...  59.9 us
    unnamed x2, local copies, waits for them, and re-layouts  1.31 us

profile of v5, /device:TPU:1, one launch (start us, length us, event | category | flops | bytes accessed | tf_op | source)
XLA Modules:
  0.0 63.2 jit_solution(17138133435731201760)
XLA Ops:
  1.9 59.9 %shard_map.113 = (bf16[128,512]{1,0:T(8,128)(2,1)S(1)}, bf16[128,512]{1,0:T(8,128)(2,1)S(1)}) custom-call(bf16[128,512]{1,0:T(8,128)(2,1)} %bitcast.12, f32[1,512]{1,0:T(1,128)} %bitcast.15, bf16[27,16,32]{2,1,0:T(8,128)(2,1)} %bitcast.14, bf16[128,512]{1,0:T(8,128)(2,1)} %bitcast.13, s32[1]{0:T(128)S(6)} %copy.16.count_ref, s32[1]{0:T(128)S(6)} %copy.17.starts_ref, ...), custom_call_target="tpu_custom_call" | custom-call | flops 7200000000 | bytes 20000000 | tf_op jit(solution)/shard_map/pallas_call | solution.py:525
  61.9 0.7 %copy.18 = bf16[1,4,1,4,8,512]{5,4,3,2,1,0:T(8,128)(2,1)} copy(bf16[1,4,1,4,8,512]{5,4,3,2,1,0:T(8,128)(2,1)S(1)} %bitcast.11) | data formatting | bytes 262144
  62.5 0.7 %copy.19 = bf16[1,4,1,4,8,512]{5,4,3,2,1,0:T(8,128)(2,1)} copy(bf16[1,4,1,4,8,512]{5,4,3,2,1,0:T(8,128)(2,1)S(1)} %bitcast.10) | data formatting | bytes 262144

commit v6 on v5

--- a/solution.py
+++ b/solution.py
@@ -353,9 +353,9 @@
     w_layout(0)
     arrived(trecv, t_r.at[0])
     a_start(1, jnp.concatenate([halo, (trecv[...].astype(F32) * source).astype(BF16)], axis=0))
+    y_relay(1)
     x_pass(5)
     x_pass(6)
-    y_relay(1)
     for k in range(7):
         x_arrived(k, 1 - CHUNKS[k][2])
     w_layout(-1)

time: 63.3 us -> 63.1 us (level)
  no operation moved by 1% of the time
where the time goes in v6:
time: 63.1 us; the launch traced here: 62.9 us
  Pallas kernels  59.7 us (95%)
  between operations  1.93 us (3%)
  local copies, waits for them, and re-layouts  1.31 us (2%)
    pallas_call x1, Pallas kernels, per_device(): pl.pallas_call(body, out_shape=[jax.ShapeDtypeStruct((128, 512), BF16)] *...  59.7 us
    unnamed x2, local copies, waits for them, and re-layouts  1.31 us

profile of v6, /device:TPU:1, one launch (start us, length us, event | category | flops | bytes accessed | tf_op | source)
XLA Modules:
  0.0 62.9 jit_solution(15454223837342617437)
XLA Ops:
  1.9 59.7 %shard_map.113 = (bf16[128,512]{1,0:T(8,128)(2,1)S(1)}, bf16[128,512]{1,0:T(8,128)(2,1)S(1)}) custom-call(bf16[128,512]{1,0:T(8,128)(2,1)} %bitcast.12, f32[1,512]{1,0:T(1,128)} %bitcast.15, bf16[27,16,32]{2,1,0:T(8,128)(2,1)} %bitcast.14, bf16[128,512]{1,0:T(8,128)(2,1)} %bitcast.13, s32[1]{0:T(128)S(6)} %copy.16.count_ref, s32[1]{0:T(128)S(6)} %copy.17.starts_ref, ...), custom_call_target="tpu_custom_call" | custom-call | flops 7200000000 | bytes 20000000 | tf_op jit(solution)/shard_map/pallas_call | solution.py:525
  61.6 0.7 %copy.18 = bf16[1,4,1,4,8,512]{5,4,3,2,1,0:T(8,128)(2,1)} copy(bf16[1,4,1,4,8,512]{5,4,3,2,1,0:T(8,128)(2,1)S(1)} %bitcast.11) | data formatting | bytes 262144
  62.3 0.7 %copy.19 = bf16[1,4,1,4,8,512]{5,4,3,2,1,0:T(8,128)(2,1)} copy(bf16[1,4,1,4,8,512]{5,4,3,2,1,0:T(8,128)(2,1)S(1)} %bitcast.10) | data formatting | bytes 262144
